TPU v7x, 512 devices: a whole 4x4x16 slice. The times are simulated.
512 devices in a mesh: gx: 8 (over x, core), gy: 8 (over z_lo), gz: 8 (over y, z_hi).
Axes of the slice: x: 4, y: 4, z: 16 (z_hi: 2, z_lo: 8; z = z_hi * 8 + z_lo), core: 2. Of those that a mesh axis runs over, the one named last changes fastest.
Arguments:
- hidden: bfloat16 [1024, 26624], P(('gz', 'gy'), 'gx'), may hold values from -16 to 16
- out_grad: bfloat16 [1024, 16384], P(('gz', 'gx'), 'gy'), may hold values from -16 to 16
- weight: bfloat16 [26624, 16384], P('gx', ('gy', 'gz')), may hold values from -0.0390625 to 0.0390625
- adapter_down_factor: bfloat16 [26624, 16], P('gx'), may hold values from -0.109375 to 0.109375
- adapter_up_factor: bfloat16 [16, 16384], P(None, 'gy'), may hold values from -0.125 to 0.125
Outputs:
- hidden_gradient: bfloat16 [1024, 26624], P(('gz', 'gy'), 'gx')
- recomputed: bfloat16 [1024, 16384], P(('gz', 'gx'), 'gy')
- grad_down: float32 [26624, 16], P(('gx', 'gz'))
- grad_up: float32 [16, 16384], P(None, ('gy', 'gz'))
All inputs are finite; a program needn't handle non-finite values.
Results may differ from a plain program's by a relative error of at most 0.017.
Values may be sent and summed in bfloat16 or wider, within the bound.
A program may use at most 64 MiB of HBM per device.

v0:
```python
import jax
import jax.numpy as jnp
from jax import lax
from jax.sharding import PartitionSpec as P

adapter_scale = 2.0


def contract_trailing(left, right):
    return lax.dot_general(
        left, right, (((1,), (1,)), ((), ())), preferred_element_type=jnp.float32
    )


def contract_first(left, right):
    return lax.dot_general(
        left, right, (((0,), (0,)), ((), ())), preferred_element_type=jnp.float32
    )


def shards(hidden, out_grad, weight, adapter_down_factor, adapter_up_factor):
    hidden_slab = lax.all_gather(hidden, "gy", axis=0, tiled=True)
    grad_slab = lax.all_gather(out_grad, "gx", axis=0, tiled=True)
    local_tokens = hidden_slab.shape[0]
    down_term = contract_trailing(grad_slab, adapter_up_factor)
    up_term = jnp.dot(hidden_slab, adapter_down_factor, preferred_element_type=jnp.float32)
    down_total = lax.psum(down_term, "gy")
    up_total = lax.psum(up_term, "gx")
    down_lowrank = down_total.astype(jnp.bfloat16)
    up_lowrank = up_total.astype(jnp.bfloat16)
    weight_full = lax.all_gather(weight, "gz", axis=1, tiled=True)
    input_term = contract_trailing(grad_slab, weight_full)
    output_term = jnp.dot(hidden_slab, weight_full, preferred_element_type=jnp.float32)
    input_combined = lax.psum_scatter(
        input_term.astype(jnp.bfloat16), "gy", scatter_dimension=0, tiled=True
    ).astype(jnp.float32)
    input_share = input_combined.shape[0]
    down_factor_rows = lax.dynamic_slice_in_dim(
        down_lowrank, lax.axis_index("gy") * input_share, input_share, 0
    )
    hidden_gradient = (
        input_combined + adapter_scale * contract_trailing(down_factor_rows, adapter_down_factor)
    ).astype(jnp.bfloat16)
    output_combined = lax.psum_scatter(
        output_term.astype(jnp.bfloat16), "gx", scatter_dimension=0, tiled=True
    ).astype(jnp.float32)
    output_share = output_combined.shape[0]
    up_factor_rows = lax.dynamic_slice_in_dim(
        up_lowrank, lax.axis_index("gx") * output_share, output_share, 0
    )
    recomputed = (
        output_combined
        + adapter_scale
        * jnp.dot(up_factor_rows, adapter_up_factor, preferred_element_type=jnp.float32)
    ).astype(jnp.bfloat16)
    grad_down_term = contract_first(hidden_slab, down_lowrank)
    grad_up_term = contract_first(up_lowrank, grad_slab)
    grad_down_sum, grad_up_sum = (
        lax.psum_scatter(
            grad_down_term.astype(jnp.bfloat16), "gz", scatter_dimension=0, tiled=True
        ).astype(jnp.float32),
        lax.psum_scatter(
            grad_up_term.astype(jnp.bfloat16), "gz", scatter_dimension=1, tiled=True
        ).astype(jnp.float32),
    )
    factor_matrix = adapter_scale / (local_tokens * lax.axis_size("gz"))
    return (hidden_gradient, recomputed, grad_down_sum * factor_matrix, grad_up_sum * factor_matrix)


def solution(mesh):
    placed = (
        P(("gz", "gy"), "gx"),
        P(("gz", "gx"), "gy"),
        P("gx", ("gy", "gz")),
        P("gx", None),
        P(None, "gy"),
    )
    return jax.shard_map(
        shards,
        mesh=mesh,
        in_specs=placed,
        out_specs=(
            P(("gz", "gy"), "gx"),
            P(("gz", "gx"), "gy"),
            P(("gx", "gz"), None),
            P(None, ("gy", "gz")),
        ),
        check_vma=False,
    )
```

profile of v0, /device:TPU:1, one launch (start us, length us, event | category | flops | bytes accessed | tf_op | source)
XLA Modules:
  0.0 808.8 jit_solution(15045729862728228244)
XLA Ops:
  7.2 0.0 copy-start
  7.2 0.0 all-gather.2.cloned.1.call-start
  7.2 0.7 all-gather.2.cloned.1.call-update
  7.9 0.0 reduce-scatter.11.cloned.1.call-start
  8.0 84.0 %all_gather.11 = bf16[128,3328]{1,0:T(8,128)(2,1)S(1)} all-gather(bf16[16,3328]{1,0:T(8,128)(2,1)} %param.5), channel_id=1, replica_groups=mesh['gx'=8,'gy'=8,'gz'=8] {'gy'}, dimensions={0}, use_global_device_ids=true | all-gather | bytes 958464 | tf_op jit(solution)/shard_map/all_gather | solution.py:22
  91.9 0.3 fusion.10
  92.2 23.5 %psum.15 = bf16[128,16]{0,1:T(8,128)(2,1)S(1)} all-reduce(f32[128,16]{0,1:T(8,128)S(1)} %fusion.10), channel_id=1, replica_groups=mesh['gx'=8,'gy'=8,'gz'=8] {'gx'}, use_global_device_ids=true, to_apply=%region_3.0 | all-reduce | flops 2048 | bytes 12288 | tf_op jit(solution)/shard_map/psum | solution.py:28
  115.8 13.3 %all_gather.9 = bf16[128,2048]{1,0:T(8,128)(2,1)S(1)} all-gather(bf16[16,2048]{1,0:T(8,128)(2,1)} %param.6), channel_id=1, replica_groups=mesh['gx'=8,'gy'=8,'gz'=8] {'gx'}, dimensions={0}, use_global_device_ids=true | all-gather | bytes 589824 | tf_op jit(solution)/shard_map/all_gather | solution.py:23
  129.1 0.8 convolution_convert_fusion.3
  129.9 0.0 reduce-scatter.11.cloned.1.call-update
  129.9 0.0 reduce-scatter.13.cloned.1.call-start
  130.0 1.1 fusion.9
  131.1 57.6 %psum.14 = bf16[128,16]{0,1:T(8,128)(2,1)S(1)} all-reduce(f32[128,16]{0,1:T(8,128)S(1)} %fusion.9), channel_id=1, replica_groups=mesh['gx'=8,'gy'=8,'gz'=8] {'gy'}, use_global_device_ids=true, to_apply=%region_1.0 | all-reduce | flops 2048 | bytes 12288 | tf_op jit(solution)/shard_map/psum | solution.py:27
  188.6 0.2 fusion.2
  188.9 1.2 copy.9
  190.1 0.0 reduce-scatter.13.cloned.1.call-update
  190.1 0.0 reduce-scatter.9.cloned.1.call-start
  190.2 290.3 %all-gather.2.cloned.1.call-done = bf16[3328,2048]{1,0:T(8,128)(2,1)} async-done(((bf16[3328,256]{1,0:T(8,128)(2,1)}), bf16[3328,2048]{1,0:T(8,128)(2,1)}) %all-gather.2.cloned.1.call-update) | async-done | bytes 13631504 | tf_op jit(solution)/shard_map/all_gather | solution.py:31
  480.5 7.8 convolution_convert_fusion.2
  488.3 0.0 reduce-scatter.9.cloned.1.call-update
  488.3 0.0 reduce-scatter.7.cloned.1.call-start
  488.4 10.4 %convolution_convert_fusion = bf16[128,3328]{1,0:T(8,128)(2,1)} fusion(bf16[128,2048]{1,0:T(8,128)(2,1)S(1)} %all_gather.9, bf16[3328,2048]{1,0:T(8,128)(2,1)} %all-gather.2.cloned.1.call-done), kind=kOutput, calls=%fused_computation | convolution fusion | flops 1745256448 | bytes 15007744 | tf_op jit(solution)/shard_map/dot_general | solution.py:10
  498.8 0.0 reduce-scatter.7.cloned.1.call-update
  498.8 92.0 %reduce-scatter.11.cloned.1.call-done = bf16[16,256]{1,0:T(8,128)(2,1)} async-done(((bf16[16,2048]{1,0:T(8,128)(2,1)}), bf16[16,256]{1,0:T(8,128)(2,1)}) %reduce-scatter.11.cloned.1.call-update) | async-done | bytes 8208 | tf_op jit(solution)/shard_map/reduce_scatter | solution.py:62
  590.8 1.3 convert_multiply_fusion.1
  592.1 111.6 %reduce-scatter.13.cloned.1.call-done = bf16[416,16]{1,0:T(8,128)(2,1)} async-done(((bf16[3328,16]{1,0:T(8,128)(2,1)}), bf16[416,16]{1,0:T(8,128)(2,1)}) %reduce-scatter.13.cloned.1.call-update) | async-done | bytes 13328
  703.7 1.0 copy.10
  704.7 0.6 convert_multiply_fusion
  705.3 30.7 %reduce-scatter.9.cloned.1.call-done = bf16[16,2048]{1,0:T(8,128)(2,1)} async-done(((bf16[128,2048]{1,0:T(8,128)(2,1)}), bf16[16,2048]{1,0:T(8,128)(2,1)}) %reduce-scatter.9.cloned.1.call-update) | async-done | bytes 65552 | tf_op jit(solution)/shard_map/reduce_scatter | solution.py:44
  736.0 1.7 fusion.4
  737.7 62.7 %reduce-scatter.7.cloned.1.call-done = bf16[16,3328]{1,0:T(8,128)(2,1)} async-done(((bf16[128,3328]{1,0:T(8,128)(2,1)}), bf16[16,3328]{1,0:T(8,128)(2,1)}) %reduce-scatter.7.cloned.1.call-update) | async-done | bytes 106512 | tf_op jit(solution)/shard_map/reduce_scatter | solution.py:34
  800.4 1.8 fusion.1
  (3 shorter events, 0.0 us)
Async XLA Ops:
  7.2 84.8 %copy-start = (bf16[3328,16]{0,1:T(8,128)(2,1)S(1)}, bf16[3328,16]{0,1:T(8,128)(2,1)}, u32[]{:S(2)}) copy-start(bf16[3328,16]{0,1:T(8,128)(2,1)} %param.8) | copy-start | bytes 319492
  7.2 473.3 %all-gather.2.cloned.1.call-start = ((), (), s32[]{:S(2)}) async-start(), calls=%async_computation.4 | async-start | bytes 15335424 | tf_op jit(solution)/shard_map/all_gather | solution.py:31
  7.9 582.9 %reduce-scatter.11.cloned.1.call-start = ((), (), s32[]{:S(2)}) async-start(), calls=%async_computation.7 | async-start | bytes 73728 | tf_op jit(solution)/shard_map/reduce_scatter | solution.py:62
  129.9 573.8 %reduce-scatter.13.cloned.1.call-start = ((), (), s32[]{:S(2)}) async-start(), calls=%async_computation.8 | async-start | bytes 958464
  190.1 545.9 %reduce-scatter.9.cloned.1.call-start = ((), (), s32[]{:S(2)}) async-start(), calls=%async_computation.6 | async-start | bytes 589824 | tf_op jit(solution)/shard_map/reduce_scatter | solution.py:44
  488.3 247.7 %copy-start.1 = (bf16[16,2048]{1,0:T(8,128)(2,1)S(1)}, bf16[16,2048]{1,0:T(8,128)(2,1)}, u32[]{:S(2)}) copy-start(bf16[16,2048]{1,0:T(8,128)(2,1)} %param.9) | copy-start | bytes 196612
  488.3 312.1 %reduce-scatter.7.cloned.1.call-start = ((), (), s32[]{:S(2)}) async-start(), calls=%async_computation.5 | async-start | bytes 958464 | tf_op jit(solution)/shard_map/reduce_scatter | solution.py:34
Sparse Core Ops, SparseCore 0:
  11.1 469.3 all-gather.1
  485.3 105.4 reduce-scatter.10
  596.0 107.6 reduce-scatter.12
  706.6 29.3 reduce-scatter.8
  738.7 61.7 reduce-scatter.6
where the time goes:
time: 813 us; the launch traced here: 809 us
  waiting for transfers between devices  588 us (72%)
  blocking collectives  178 us (22%)
  matrix products  24.2 us (3%)
  between operations  13.8 us (2%)
    all_gather x1, waiting for transfers between devices, shards(): weight_full = lax.all_gather(weight, 'gz', axis=1, tiled=True)  290 us
    unnamed x6, waiting for transfers between devices  112 us
    reduce_scatter x1, waiting for transfers between devices, shards(): lax.psum_scatter(grad_up_term.astype(jnp.bfloat16), 'gz', scatter_dimensi...  92 us
    all_gather x1, blocking collectives, shards(): hidden_slab = lax.all_gather(hidden, 'gy', axis=0, tiled=True)  84 us
    reduce_scatter x1, waiting for transfers between devices, shards(): lax.psum_scatter(input_term.astype(jnp.bfloat16), 'gy', scatter_dimension...  62.7 us
    psum x1, blocking collectives, shards(): down_total = lax.psum(down_term, 'gy')  57.6 us
    reduce_scatter x1, waiting for transfers between devices, shards(): lax.psum_scatter(output_term.astype(jnp.bfloat16), 'gx', scatter_dimensio...  30.7 us
    psum x1, blocking collectives, shards(): up_total = lax.psum(up_term, 'gx')  23.5 us
  transfers between devices with their start and end apart: 5, of which 5 were waited for; matrix products, arithmetic and copies ran while one was open for 3% of the time, Pallas kernels for 0%

commit v1 on v0

v1 whole, which is shorter than its diff:
```python
import functools

import jax
import jax.numpy as jnp
from jax import lax
from jax.experimental import pallas as pl
from jax.experimental.pallas import tpu as pltpu
from jax.sharding import PartitionSpec as P

MESH = pl.DeviceIdType.MESH
BF = jnp.bfloat16
F32 = jnp.float32

FF = 3328
UNIT = 256
UNITS = FF // UNIT
HALF = UNIT // 2
TOK = 256
FEAT = 1024
AHEAD = 3
WIN = 512


def nt(left, right):
    return lax.dot_general(left, right, (((1,), (1,)), ((), ())), preferred_element_type=F32)


def nn(left, right):
    return jnp.dot(left, right, preferred_element_type=F32)


def mod(value, size):
    return lax.rem(value + size, size)


def rows16(block):
    return pl.ds(pl.multiple_of(block * 16, 16), 16)


def unit_cols(unit):
    return pl.ds(pl.multiple_of(unit * UNIT, UNIT), UNIT)


def kernel(
    hid, og, w, ad, au,
    hg, rec, gd, gu,
    W, H, G, I, O, Ob, plus, minus, AD, ADT, AU, PD, PU, DT, UT, GDs, GDr, GUs, GUr, OX, OPs, OPr,
    lsem, wds, wdr, wfs, wfr, hs, hr, gzs, gzr, gxs, gxr, pds, pdr, pus, pur, gys, gyr,
    rps, rpr, rms, rmr, oxs, oxr, ops_, opr,
):
    gx, gy, gz = lax.axis_index("gx"), lax.axis_index("gy"), lax.axis_index("gz")
    y, zh = lax.div(gz, 2), lax.rem(gz, 2)
    z = zh * 8 + gy

    def zdev(where):
        return {"gy": lax.rem(where, 8), "gz": y * 2 + lax.div(where, 8)}

    def ydev(where):
        return {"gz": where * 2 + zh}

    zup, zdown = zdev(mod(z + 1, 16)), zdev(mod(z - 1, 16))
    yup, ydown = mod(y + 1, 4), mod(y - 1, 4)
    yfar = mod(y + 2, 4)
    partner = {"gz": y * 2 + (1 - zh)}

    def remote(src, dst, ssem, rsem, to):
        return pltpu.make_async_remote_copy(
            src_ref=src, dst_ref=dst, send_sem=ssem, recv_sem=rsem, device_id=to, device_id_type=MESH
        )

    my_cols = pl.ds(pl.multiple_of(y * 256, 256), 256)

    def quarter(q, which):
        return pl.ds(pl.multiple_of((2 * q + which) * 256, 256), 256)

    mine = rows16(zh * 8 + gx)
    theirs = rows16((1 - zh) * 8 + gx)
    loads = [
        pltpu.make_async_copy(hid, H.at[rows16(z), :], lsem.at[0]),
        pltpu.make_async_copy(w, W.at[:, my_cols], lsem.at[1]),
        pltpu.make_async_copy(ad, AD, lsem.at[2]),
    ]
    for q in range(4):
        loads.append(pltpu.make_async_copy(og.at[:, quarter(q, zh)], G.at[mine, q * 256:(q + 1) * 256], lsem.at[3 + q]))
        loads.append(pltpu.make_async_copy(au.at[:, quarter(q, zh)], AU.at[:, q * 256:(q + 1) * 256], lsem.at[7 + q]))
    for load in loads:
        load.start()

    barrier = pltpu.get_barrier_semaphore()
    peers = [zup, zdown, partner, ydev(yup), ydev(ydown), ydev(yfar)]
    peers += [{"gx": mod(gx + i, 8)} for i in range(1, 8)]
    for peer in peers:
        pl.semaphore_signal(barrier, inc=1, device_id=peer, device_id_type=MESH)
    pl.semaphore_wait(barrier, len(peers))

    def w_rows(unit):
        return pl.ds(pl.multiple_of(unit * UNIT, UNIT), UNIT)

    def w_first(unit):
        return pl.ds(pl.multiple_of(unit * UNIT, HALF), HALF)

    def w_second(unit):
        return pl.ds(pl.multiple_of(unit * UNIT + HALF, HALF), HALF)

    def cols_of(where):
        return pl.ds(pl.multiple_of(where * 256, 256), 256)

    def w_direct(unit, side):
        return remote(
            w.at[w_rows(unit), :], W.at[w_rows(unit), my_cols], wds.at[side, unit], wdr.at[side, unit],
            ydev(yup if side == 0 else ydown),
        )

    def w_arrived(unit, side):
        part = W.at[w_rows(unit), cols_of(ydown if side == 0 else yup)]
        return remote(part, part, wds.at[side, unit], wdr.at[side, unit], ydev(yup))

    def w_pass(unit, side):
        part = W.at[w_first(unit) if side == 0 else w_second(unit), cols_of(ydown if side == 0 else yup)]
        return remote(part, part, wfs.at[side, unit], wfr.at[side, unit], ydev(yup if side == 0 else ydown))

    def w_passed(unit, side):
        part = W.at[w_first(unit) if side == 0 else w_second(unit), cols_of(yfar)]
        return remote(part, part, wfs.at[side, unit], wfr.at[side, unit], ydev(yup))

    def w_step(unit):
        @pl.when(unit + AHEAD < UNITS)
        def _():
            w_direct(unit + AHEAD, 0).start()
            w_direct(unit + AHEAD, 1).start()

        for side in range(2):
            w_arrived(unit, side).wait_recv()
            w_pass(unit, side).start()

    for unit in range(AHEAD):
        w_direct(unit, 0).start()
        w_direct(unit, 1).start()

    for q in range(4):
        remote(og.at[:, quarter(q, 1 - zh)], G.at[mine, q * 256:(q + 1) * 256], gzs, gzr, partner).start()

    def h_move(step, side):
        part = H.at[rows16(mod(z - step if side == 0 else z + step, 16)), :]
        return remote(part, part, hs.at[side, step], hr.at[side, step], zup if side == 0 else zdown)

    def h_got(step, side):
        part = H.at[rows16(mod(z - 1 - step if side == 0 else z + 1 + step, 16)), :]
        return remote(part, part, hs.at[side, step], hr.at[side, step], zup)

    def h_step(step):
        h_got(step, 0).wait_recv()
        if step < 7:
            h_move(step + 1, 0).start()
            h_got(step, 1).wait_recv()
        if step < 6:
            h_move(step + 1, 1).start()

    loads[0].wait()
    h_move(0, 0).start()
    h_move(0, 1).start()

    def g_send(i, rows, which):
        return remote(G.at[rows, :], G.at[rows, :], gxs.at[which], gxr.at[which], {"gx": mod(gx + i, 8)})

    for load in loads[3:]:
        load.wait()
    for i in range(1, 8):
        g_send(i, mine, 0).start()
    w_step(0)
    h_step(0)
    remote(G.at[theirs, :], G.at[theirs, :], gzs, gzr, partner).wait_recv()
    for i in range(1, 8):
        g_send(i, theirs, 1).start()
    h_step(1)
    w_step(1)
    h_step(2)
    h_step(3)
    w_step(2)
    h_step(4)
    loads[2].wait()
    eye = (lax.broadcasted_iota(jnp.int32, (16, 16), 0) == lax.broadcasted_iota(jnp.int32, (16, 16), 1)).astype(BF)

    def transpose_unit(unit, _):
        ADT[:, unit_cols(unit)] = nt(eye, AD[w_rows(unit), :]).astype(BF)
        return 0

    lax.fori_loop(0, UNITS, transpose_unit, 0)
    h_step(5)

    for which in range(2):
        part = G.at[0:112, :]
        remote(part, part, gxs.at[which], gxr.at[which], {"gx": mod(gx + 1, 8)}).wait_recv()
    PD[pl.ds(z, 1)] = nt(AU[...], G[...]).reshape(1, 16, TOK)

    def pd_move(step, side):
        part = PD.at[mod(z - step if side == 0 else z + step, 16)]
        return remote(part, part, pds.at[side, step], pdr.at[side, step], zup if side == 0 else zdown)

    def pd_got(step, side):
        part = PD.at[mod(z - 1 - step if side == 0 else z + 1 + step, 16)]
        return remote(part, part, pds.at[side, step], pdr.at[side, step], zup)

    pd_move(0, 0).start()
    pd_move(0, 1).start()
    w_step(3)
    h_step(6)
    h_step(7)

    def up_unit(unit, total):
        return total + nt(ADT[:, unit_cols(unit)], H[:, unit_cols(unit)])

    PU[pl.ds(gx, 1)] = lax.fori_loop(0, UNITS, up_unit, jnp.zeros((16, TOK), F32)).reshape(1, 16, TOK)

    def pu_send(i):
        return remote(PU.at[gx], PU.at[gx], pus.at[i - 1], pur.at[i - 1], {"gx": mod(gx + i, 8)})

    def pu_got(i):
        part = PU.at[mod(gx - i, 8)]
        return remote(part, part, pus.at[i - 1], pur.at[i - 1], {"gx": mod(gx + i, 8)})

    for i in range(1, 8):
        pu_send(i).start()

    O[...] = jnp.zeros_like(O)
    loads[1].wait()

    def compute(unit):
        for side in range(2):
            w_passed(unit, side).wait_recv()
        block = W[w_rows(unit), :]
        I[:, unit_cols(unit)] = nt(G[...], block).astype(BF)
        O[...] += nn(H[:, unit_cols(unit)], block)

    def pick(block):
        return (
            lax.broadcasted_iota(jnp.int32, (16, TOK), 1)
            == lax.broadcasted_iota(jnp.int32, (16, TOK), 0) + block * 16
        ).astype(BF)

    def ring_plus(k, unit):
        cols = unit_cols(unit)
        if k == 0:
            src = I.at[rows16(mod(z + 8, 16)), cols]
        else:
            part = plus.at[k - 1, :, cols]
            remote(part, part, rps.at[k - 1, unit], rpr.at[k - 1, unit], zup).wait_recv()
            plus[k - 1, :, cols] = (
                plus[k - 1, :, cols].astype(F32) + I[rows16(mod(z + 8 - k, 16)), cols].astype(F32)
            ).astype(BF)
            src = part
        remote(src, plus.at[k, :, cols], rps.at[k, unit], rpr.at[k, unit], zup).start()

    def ring_minus(k, unit):
        cols = unit_cols(unit)
        if k == 0:
            src = I.at[rows16(mod(z - 7, 16)), cols]
        else:
            part = minus.at[k - 1, :, cols]
            remote(part, part, rms.at[k - 1, unit], rmr.at[k - 1, unit], zdown).wait_recv()
            minus[k - 1, :, cols] = (
                minus[k - 1, :, cols].astype(F32) + I[rows16(mod(z - 7 + k, 16)), cols].astype(F32)
            ).astype(BF)
            src = part
        remote(src, minus.at[k, :, cols], rms.at[k, unit], rmr.at[k, unit], zdown).start()

    def ring_end(unit):
        cols = unit_cols(unit)
        up, down = plus.at[7, :, cols], minus.at[6, :, cols]
        remote(up, up, rps.at[7, unit], rpr.at[7, unit], zup).wait_recv()
        remote(down, down, rms.at[6, unit], rmr.at[6, unit], zdown).wait_recv()
        total = plus[7, :, cols].astype(F32) + minus[6, :, cols].astype(F32) + I[rows16(z), cols].astype(F32)
        low = nt(pick(z), DT[...]).astype(BF)
        hg[:, cols] = (total + 2.0 * nn(low, ADT[:, cols])).astype(BF)

    def window(where):
        block = 2 * where + zh
        return pl.ds(pl.multiple_of(lax.div(block * 13, 4) * 128, 128), WIN)

    def gy_send(kind, i):
        src, dst = (GDs.at[i], GDr.at[i - 1]) if kind == 0 else (GUs.at[i], GUr.at[i - 1])
        return remote(src, dst, gys.at[kind, i - 1], gyr.at[kind, i - 1], ydev(mod(y + i, 4)))

    def ox_rows(which):
        return rows16(which * 8 + gx)

    def ox_send(i, which):
        to = mod(gx + i, 8)
        return remote(
            Ob.at[rows16(which * 8 + to), :], OX.at[i, which], oxs, oxr, {"gx": to}
        )

    def loop(i, _):
        for at, unit in ((1, 4), (3, 5), (4, 6)):
            @pl.when(i == at)
            def _(unit=unit):
                w_step(jnp.int32(unit))

        @pl.when((i >= 6) & (i < 12))
        def _():
            w_step(i + 1)

        @pl.when(i < UNITS)
        def _():
            compute(i)

        for step in range(8):
            @pl.when(i == step)
            def _(step=step):
                pd_got(step, 0).wait_recv()
                if step < 7:
                    pd_move(step + 1, 0).start()
                    pd_got(step, 1).wait_recv()
                if step < 6:
                    pd_move(step + 1, 1).start()

        @pl.when(i == 3)
        def _():
            for j in range(1, 8):
                pu_got(j).wait_recv()
            UT[...] = jnp.sum(PU[...], axis=0).astype(BF)
            for j in range(4):
                cols = cols_of(mod(y + j, 4))
                GUs[j] = nn(UT[...], G[:, cols])
                if j:
                    gy_send(1, j).start()

        @pl.when(i == 7)
        def _():
            DT[...] = jnp.sum(PD[...], axis=0).astype(BF)
            for j in range(4):
                GDs[j] = nn(DT[...], H[:, window(mod(y + j, 4))])
                if j:
                    gy_send(0, j).start()

        @pl.when(i >= 8)
        def _():
            ring_end(i - 8)

        for k in range(7, -1, -1):
            @pl.when((i - k >= 0) & (i - k < UNITS))
            def _(k=k):
                ring_plus(k, i - k)
                if k < 7:
                    ring_minus(k, i - k)

        @pl.when(i == UNITS - 1)
        def _():
            Ob[...] = O[...].astype(BF)
            for j in range(1, 8):
                for which in range(2):
                    ox_send(j, which).start()

        @pl.when(i == UNITS + 4)
        def _():
            part = OX.at[1:8]
            remote(part, part, oxs, oxr, zup).wait_recv()
            for which, block in ((0, 1 - zh), (1, zh)):
                total = O[ox_rows(block), :]
                for j in range(1, 8):
                    total = total + OX[j, block].astype(F32)
                low = nt(pick(block * 8 + gx), UT[...]).astype(BF)
                result = (total + 2.0 * nn(low, AU[...])).astype(BF)
                if which == 0:
                    OPs[...] = result
                    remote(OPs, OPr, ops_, opr, partner).start()
                else:
                    for q in range(4):
                        rec[:, quarter(q, zh)] = result[:, q * 256:(q + 1) * 256]

        return 0

    lax.fori_loop(0, UNITS + 8, loop, 0)

    for j in range(1, 4):
        for kind in range(2):
            gy_send(kind, j).wait_recv()
    gd[...] = (GDs[0] + GDr[0] + GDr[1] + GDr[2]) * (2.0 / 1024)
    gu[...] = (GUs[0] + GUr[0] + GUr[1] + GUr[2]) * (2.0 / 1024)

    remote(OPs, OPr, ops_, opr, partner).wait_recv()
    for q in range(4):
        rec[:, quarter(q, 1 - zh)] = OPr[:, q * 256:(q + 1) * 256]

    remote(OPs, OPr, ops_, opr, partner).wait_send()
    part = OX.at[1:8]
    remote(part, part, oxs, oxr, zup).wait_send()
    remote(G.at[mine, :], G.at[mine, :], gzs, gzr, partner).wait_send()
    for which in range(2):
        remote(G.at[0:112, :], G.at[0:112, :], gxs.at[which], gxr.at[which], zup).wait_send()
    for j in range(1, 8):
        pu_send(j).wait_send()
    for j in range(1, 4):
        for kind in range(2):
            gy_send(kind, j).wait_send()
    for step in range(8):
        for side in range(2 if step < 7 else 1):
            h_move(step, side).wait_send()
            pd_move(step, side).wait_send()

    def finish(unit, _):
        for side in range(2):
            w_direct(unit, side).wait_send()
            w_pass(unit, side).wait_send()
        cols = unit_cols(unit)
        for k in range(8):
            remote(plus.at[k, :, cols], plus.at[k, :, cols], rps.at[k, unit], rpr.at[k, unit], zup).wait_send()
            if k < 7:
                remote(minus.at[k, :, cols], minus.at[k, :, cols], rms.at[k, unit], rmr.at[k, unit], zdown).wait_send()
        return 0

    lax.fori_loop(0, UNITS, finish, 0)


def shards(hidden, out_grad, weight, adapter_down_factor, adapter_up_factor):
    any_spec = pl.BlockSpec(memory_space=pl.ANY)
    vmem_spec = pl.BlockSpec(memory_space=pltpu.VMEM)
    dma = pltpu.SemaphoreType.DMA
    hg, rec, gd, gu = pl.pallas_call(
        kernel,
        out_shape=(
            jax.ShapeDtypeStruct((16, FF), BF),
            jax.ShapeDtypeStruct((16, 2048), BF),
            jax.ShapeDtypeStruct((16, WIN), F32),
            jax.ShapeDtypeStruct((16, 256), F32),
        ),
        in_specs=[any_spec] * 5,
        out_specs=(vmem_spec,) * 4,
        scratch_shapes=[
            pltpu.VMEM((FF, FEAT), BF),
            pltpu.VMEM((TOK, FF), BF),
            pltpu.VMEM((TOK, FEAT), BF),
            pltpu.VMEM((TOK, FF), BF),
            pltpu.VMEM((TOK, FEAT), F32),
            pltpu.VMEM((TOK, FEAT), BF),
            pltpu.VMEM((8, 16, FF), BF),
            pltpu.VMEM((7, 16, FF), BF),
            pltpu.VMEM((FF, 16), BF),
            pltpu.VMEM((16, FF), BF),
            pltpu.VMEM((16, FEAT), BF),
            pltpu.VMEM((16, 16, TOK), F32),
            pltpu.VMEM((8, 16, TOK), F32),
            pltpu.VMEM((16, TOK), BF),
            pltpu.VMEM((16, TOK), BF),
            pltpu.VMEM((4, 16, WIN), F32),
            pltpu.VMEM((3, 16, WIN), F32),
            pltpu.VMEM((4, 16, 256), F32),
            pltpu.VMEM((3, 16, 256), F32),
            pltpu.VMEM((8, 2, 16, FEAT), BF),
            pltpu.VMEM((16, FEAT), BF),
            pltpu.VMEM((16, FEAT), BF),
            dma((11,)),
            dma((2, UNITS)), dma((2, UNITS)),
            dma((2, UNITS)), dma((2, UNITS)),
            dma((2, 8)), dma((2, 8)),
            dma, dma,
            dma((2,)), dma((2,)),
            dma((2, 8)), dma((2, 8)),
            dma((7,)), dma((7,)),
            dma((2, 3)), dma((2, 3)),
            dma((8, UNITS)), dma((8, UNITS)),
            dma((7, UNITS)), dma((7, UNITS)),
            dma, dma,
            dma, dma,
        ],
        compiler_params=pltpu.CompilerParams(
            collective_id=0, has_side_effects=True, vmem_limit_bytes=48 * 1024 * 1024
        ),
    )(hidden, out_grad, weight, adapter_down_factor, adapter_up_factor)
    offset = lax.rem(lax.axis_index("gz"), 4) * 32
    grad_down = lax.dynamic_slice_in_dim(gd, offset, FF // 8, 1).T
    return hg, rec, grad_down, gu


def solution(mesh):
    placed = (
        P(("gz", "gy"), "gx"),
        P(("gz", "gx"), "gy"),
        P("gx", ("gy", "gz")),
        P("gx", None),
        P(None, "gy"),
    )
    return jax.shard_map(
        shards,
        mesh=mesh,
        in_specs=placed,
        out_specs=(
            P(("gz", "gy"), "gx"),
            P(("gz", "gx"), "gy"),
            P(("gx", "gz"), None),
            P(None, ("gy", "gz")),
        ),
        check_vma=False,
    )
```

time: 813 us -> 140 us (0.17)
  the two profiles are of different devices: /device:TPU:1 before, /device:TPU:4 now
where the time goes in v1:
time: 140 us; the launch traced here: 139 us
  Pallas kernels  131 us (94%)
  local copies, waits for them, and re-layouts  7.91 us (6%)
    pallas_call x1, Pallas kernels, shards(): pl.pallas_call(kernel, out_shape=(jax.ShapeDtypeStruct((16, FF), BF), jax...  131 us
    unnamed x12, local copies, waits for them, and re-layouts  7.22 us

profile of v1, /device:TPU:4, one launch (start us, length us, event | category | flops | bytes accessed | tf_op | source)
XLA Modules:
  0.0 139.3 jit_solution(1498721883114653)
XLA Ops:
  0.6 1.3 copy.9.ad
  1.9 0.0 copy-start
  2.0 1.4 %copy-done = bf16[3328,256]{1,0:T(8,128)(2,1)S(1)} copy-done((bf16[3328,256]{1,0:T(8,128)(2,1)S(1)}, bf16[3328,256]{1,0:T(8,128)(2,1)}, u32[]{:S(2)}) %copy-start) | copy-done | bytes 1703960
  3.4 0.0 copy-start.1
  3.4 0.9 copy-done.1
  4.3 0.0 copy-start.2
  4.3 0.8 copy-done.2
  5.1 0.0 copy-start.3
  5.1 0.8 copy-done.3
  6.0 130.7 %shard_map.84 = (bf16[16,3328]{1,0:T(8,128)(2,1)S(1)}, bf16[16,2048]{1,0:T(8,128)(2,1)S(1)}, f32[16,512]{1,0:T(8,128)S(1)}, f32[16,256]{1,0:T(8,128)S(1)}) custom-call(bf16[16,3328]{1,0:T(8,128)(2,1)S(1)} %copy-done.1, bf16[16,2048]{1,0:T(8,128)(2,1)S(1)} %copy-done.2, bf16[3328,256]{1,0:T(8,128)(2,1)S(1)} %copy-done, bf16[3328,16]{1,0:T(8,128)(2,1)S(1)} %copy.9.ad, ...), custom_call_target="tpu_custom_call" | custom-call | tf_op jit(solution)/shard_map/pallas_call | solution.py:419
  136.7 0.7 dynamic-slice_bitcast_fusion
  137.4 0.6 copy.13
  138.1 0.6 copy.14
  138.7 0.6 copy.15
Async XLA Ops:
  1.9 1.5 %copy-start = (bf16[3328,256]{1,0:T(8,128)(2,1)S(1)}, bf16[3328,256]{1,0:T(8,128)(2,1)}, u32[]{:S(2)}) copy-start(bf16[3328,256]{1,0:T(8,128)(2,1)} %w.1) | copy-start | bytes 5111812
  3.4 0.9 copy-start.1
  4.3 0.8 copy-start.2
  5.1 0.8 copy-start.3

commit v2 on v0

v2 whole, which is shorter than its diff:
```python
import functools

import jax
import jax.numpy as jnp
from jax import lax
from jax.experimental import pallas as pl
from jax.experimental.pallas import tpu as pltpu
from jax.sharding import PartitionSpec as P

MESH = pl.DeviceIdType.MESH
BF = jnp.bfloat16
F32 = jnp.float32

FF = 3328
UNIT = 256
UNITS = FF // UNIT
HALF = UNIT // 2
TOK = 256
FEAT = 1024
AHEAD = 4
CLASS_LAG = 5
END_LAG = 8
WIN = 512


def nt(left, right):
    return lax.dot_general(left, right, (((1,), (1,)), ((), ())), preferred_element_type=F32)


def nn(left, right):
    return jnp.dot(left, right, preferred_element_type=F32)


def mod(value, size):
    return lax.rem(value + size, size)


def rows16(block):
    return pl.ds(pl.multiple_of(block * 16, 16), 16)


def unit_cols(unit):
    return pl.ds(pl.multiple_of(unit * UNIT, UNIT), UNIT)


def kernel(
    hid, og, w, adt, au,
    hg, rec, gd, gu,
    W, H, G, I, O, Ob, R1, R2, ADT, AU, PD, PU, DT, UT, GDs, GDr, GUs, GUr, OXn, OXf, OPs, OPr,
    lsem, wds, wdr, wfs, wfr, hs, hr, gzs, gzr, gxs, gxr, pds, pdr, pus, pur, gys, gyr,
    r1s, r1r, r2s, r2r, oxs, oxr, ops_, opr,
):
    gx, gy, gz = lax.axis_index("gx"), lax.axis_index("gy"), lax.axis_index("gz")
    y, zh = lax.div(gz, 2), lax.rem(gz, 2)
    z = zh * 8 + gy
    zc, zm = lax.rem(z, 4), lax.div(z, 4)

    def zdev(step):
        where = mod(z + step, 16)
        return {"gy": lax.rem(where, 8), "gz": y * 2 + lax.div(where, 8)}

    def ydev(where):
        return {"gz": where * 2 + zh}

    def xdev(step):
        return {"gx": mod(gx + step, 8)}

    yup, ydown, yfar = mod(y + 1, 4), mod(y - 1, 4), mod(y + 2, 4)
    partner = {"gz": y * 2 + (1 - zh)}

    def remote(src, dst, ssem, rsem, to):
        return pltpu.make_async_remote_copy(
            src_ref=src, dst_ref=dst, send_sem=ssem, recv_sem=rsem, device_id=to, device_id_type=MESH
        )

    def got(part, sem):
        remote(part, part, sem, sem, xdev(1)).wait_recv()

    def left(part, sem):
        remote(part, part, sem, sem, xdev(1)).wait_send()

    def rows_of(where):
        return rows16(lax.rem(where, 4) * 4 + lax.div(where, 4))

    def quarter(q, which):
        return pl.ds(pl.multiple_of((2 * q + which) * 256, 256), 256)

    def cols_of(where):
        return pl.ds(pl.multiple_of(where * 256, 256), 256)

    my_cols = cols_of(y)
    mine = rows_of(zh * 8 + gx)
    theirs = rows_of((1 - zh) * 8 + gx)

    loads = [
        pltpu.make_async_copy(hid, H.at[rows_of(z), :], lsem.at[0]),
        pltpu.make_async_copy(w, W.at[:, my_cols], lsem.at[1]),
        pltpu.make_async_copy(adt, ADT, lsem.at[2]),
    ]
    for q in range(4):
        loads.append(pltpu.make_async_copy(og.at[:, quarter(q, zh)], G.at[mine, q * 256:(q + 1) * 256], lsem.at[3 + q]))
        loads.append(pltpu.make_async_copy(au.at[:, quarter(q, zh)], AU.at[:, q * 256:(q + 1) * 256], lsem.at[7 + q]))
    for load in loads:
        load.start()

    barrier = pltpu.get_barrier_semaphore()
    peers = [zdev(i) for i in (1, -1, 2, -2, 4, -4, 8)] + [ydev(yup), ydev(ydown), ydev(yfar)]
    peers += [xdev(i) for i in range(1, 8)]
    for peer in peers:
        pl.semaphore_signal(barrier, inc=1, device_id=peer, device_id_type=MESH)
    pl.semaphore_wait(barrier, len(peers))

    def w_rows(unit):
        return pl.ds(pl.multiple_of(unit * UNIT, UNIT), UNIT)

    def w_half(unit, side):
        return pl.ds(pl.multiple_of(unit * UNIT + side * HALF, HALF), HALF)

    def w_direct(unit, side):
        return remote(
            w.at[w_rows(unit), :], W.at[w_rows(unit), my_cols], wds.at[side], wdr.at[side, unit],
            ydev(yup if side == 0 else ydown),
        )

    def w_pass(unit, side):
        part = W.at[w_half(unit, side), cols_of(ydown if side == 0 else yup)]
        return remote(part, part, wfs.at[side], wfr.at[side, unit], ydev(yup if side == 0 else ydown))

    def w_step(unit):
        @pl.when(unit + AHEAD < UNITS)
        def _():
            w_direct(unit + AHEAD, 0).start()
            w_direct(unit + AHEAD, 1).start()

        for side in range(2):
            got(W.at[w_rows(unit), cols_of(ydown if side == 0 else yup)], wdr.at[side, unit])
            w_pass(unit, side).start()

    for unit in range(AHEAD):
        w_direct(unit, 0).start()
        w_direct(unit, 1).start()

    for q in range(4):
        remote(og.at[:, quarter(q, 1 - zh)], G.at[mine, q * 256:(q + 1) * 256], gzs, gzr, partner).start()

    def h_move(step, side):
        part = H.at[rows_of(mod(z - step if side == 0 else z + step, 16)), :]
        return remote(part, part, hs.at[side], hr.at[side, step], zdev(1 if side == 0 else -1))

    def h_step(step):
        got(H.at[rows_of(mod(z - 1 - step, 16)), :], hr.at[0, step])

        @pl.when(step < 7)
        def _():
            h_move(step + 1, 0).start()
            got(H.at[rows_of(mod(z + 1 + step, 16)), :], hr.at[1, step])

        @pl.when(step < 6)
        def _():
            h_move(step + 1, 1).start()

    loads[0].wait()
    h_move(0, 0).start()
    h_move(0, 1).start()

    def g_send(i, rows, which):
        return remote(G.at[rows, :], G.at[rows, :], gxs.at[which], gxr.at[which], xdev(i))

    for load in loads[2:]:
        load.wait()
    for i in range(1, 8):
        g_send(i, mine, 0).start()
    O[...] = jnp.zeros_like(O)
    loads[1].wait()

    pd_steps = ((1, -1, 2), (4, -4, 8))

    def pd_send(stage, i):
        return remote(
            PD.at[stage, 0], PD.at[stage, i + 1], pds.at[stage, i], pdr.at[stage, i], zdev(pd_steps[stage][i])
        )

    def pd_sum(stage):
        for i in range(3):
            got(PD.at[stage, i + 1], pdr.at[stage, i])
        return PD[stage, 0] + PD[stage, 1] + PD[stage, 2] + PD[stage, 3]

    def pu_send(i):
        return remote(PU.at[0], PU.at[i], pus, pur.at[i - 1], xdev(i))

    def up_unit(unit, total):
        return total + nt(ADT[:, unit_cols(unit)], H[:, unit_cols(unit)])

    def window(where):
        block = 2 * where + zh
        return pl.ds(pl.multiple_of(lax.div(block * 13, 4) * 128, 128), WIN)

    def gy_send(kind, i):
        src, dst = (GDs.at[i - 1], GDr.at[i - 1]) if kind == 0 else (GUs.at[i - 1], GUr.at[i - 1])
        return remote(src, dst, gys.at[kind, i - 1], gyr.at[kind, i - 1], ydev(mod(y + i, 4)))

    class_rows = pl.ds(pl.multiple_of(zc * 64, 64), 64)

    def r1_send(unit, i):
        step = (1, -1, 2 - 4 * lax.rem(unit, 2))[i]
        rows = pl.ds(pl.multiple_of(lax.rem(z + step + 16, 4) * 64, 64), 64)
        cols = unit_cols(unit)
        return remote(I.at[rows, cols], R1.at[i, :, cols], r1s.at[i], r1r.at[i, unit], zdev(step))

    def r2_send(unit, i):
        rows = rows16(lax.rem(zm + i + 1, 4))
        cols = unit_cols(unit)
        return remote(
            R1.at[0, rows, cols], R2.at[i, :, cols], r2s.at[i], r2r.at[i, unit], zdev((4, 8, -4)[i])
        )

    def input_unit(unit):
        for side in range(2):
            got(W.at[w_half(unit, side), cols_of(yfar)], wfr.at[side, unit])
        I[:, unit_cols(unit)] = nt(G[...], W[w_rows(unit), :]).astype(BF)
        for i in range(3):
            r1_send(unit, i).start()

    def input_class(unit):
        cols = unit_cols(unit)
        for i in range(3):
            got(R1.at[i, :, cols], r1r.at[i, unit])
        total = I[class_rows, cols].astype(F32)
        for i in range(3):
            total = total + R1[i, :, cols].astype(F32)
        R1[0, :, cols] = total.astype(BF)
        for i in range(3):
            r2_send(unit, i).start()

    def pick(where):
        first = (lax.rem(where, 4) * 4 + lax.div(where, 4)) * 16
        return (
            lax.broadcasted_iota(jnp.int32, (16, TOK), 1) == lax.broadcasted_iota(jnp.int32, (16, TOK), 0) + first
        ).astype(BF)

    def input_end(unit):
        cols = unit_cols(unit)
        for i in range(3):
            got(R2.at[i, :, cols], r2r.at[i, unit])
        total = R1[0, rows16(zm), cols].astype(F32)
        for i in range(3):
            total = total + R2[i, :, cols].astype(F32)
        low = nt(pick(z), DT[...]).astype(BF)
        hg[:, cols] = (total + 2.0 * nn(low, ADT[:, cols])).astype(BF)

    order = (0, 1, 3, 2)

    def output_unit(places, unit):
        block = H[:, unit_cols(unit)]
        for q in places:
            O[:, q * 256:(q + 1) * 256] += nn(block, W[w_rows(unit), cols_of(mod(y + order[q], 4))])

    def ox_send(far, i, which):
        to = mod(gx + i, 8)
        rows = rows_of(which * 8 + to)
        src = Ob.at[rows, 768:1024] if far else Ob.at[rows, 0:768]
        return remote(src, (OXf if far else OXn).at[i, which], oxs.at[far], oxr.at[far], xdev(i))

    def ox_go(far):
        lo, hi = (768, 1024) if far else (0, 768)
        Ob[:, lo:hi] = O[:, lo:hi].astype(BF)
        for i in range(1, 8):
            for which in range(2):
                ox_send(far, i, which).start()

    def op_send(far):
        lo, hi = (768, 1024) if far else (0, 768)
        return remote(OPs.at[:, lo:hi], OPr.at[:, lo:hi], ops_.at[far], opr.at[far], partner)

    def ox_sum(far):
        lo, hi = (768, 1024) if far else (0, 768)
        OX = OXf if far else OXn
        got(OX.at[1:8], oxr.at[far])
        for which, half in ((0, 1 - zh), (1, zh)):
            total = O[rows_of(half * 8 + gx), lo:hi]
            for i in range(1, 8):
                total = total + OX[i, half].astype(F32)
            low = nt(pick(half * 8 + gx), UT[...]).astype(BF)
            for q in range(lo // 256, hi // 256):
                factor = AU[:, cols_of(mod(y + order[q], 4))]
                part = total[:, q * 256 - lo:(q + 1) * 256 - lo]
                part = (part + 2.0 * nn(low, factor)).astype(BF)
                if which == 0:
                    OPs[:, q * 256:(q + 1) * 256] = part
                else:
                    rec[:, quarter(mod(y + order[q], 4), zh)] = part
            if which == 0:
                op_send(far).start()

    def op_end(far):
        lo, hi = (768, 1024) if far else (0, 768)
        got(OPr.at[:, lo:hi], opr.at[far])
        for q in range(lo // 256, hi // 256):
            rec[:, quarter(mod(y + order[q], 4), 1 - zh)] = OPr[:, q * 256:(q + 1) * 256]

    def loop(j, _):
        @pl.when(j < 8)
        def _():
            h_step(j)

        @pl.when(j == 1)
        def _():
            got(G.at[theirs, :], gzr)
            for i in range(1, 8):
                g_send(i, theirs, 1).start()

        w_step(j)

        @pl.when(j == 2)
        def _():
            for which in range(2):
                got(G.at[0:112, :], gxr.at[which])
            PD[0, 0] = nt(AU[...], G[...])
            for i in range(3):
                pd_send(0, i).start()

        first = lax.min(3 * (j - 8), UNITS - 1)
        last = lax.min(3 * (j - 7), UNITS)

        @pl.when(j >= 8)
        def _():
            def near(unit, _):
                output_unit((0, 1, 2), unit)
                return 0

            lax.fori_loop(first, last, near, 0)

        @pl.when(j == UNITS - 1)
        def _():
            ox_go(0)

        @pl.when(j >= 2)
        def _():
            input_unit(j - 2)

        far_first = lax.min(4 * (j - 9), j - 2)
        far_last = lax.min(4 * (j - 8), j - 1)

        @pl.when(j >= 9)
        def _():
            def far(unit, _):
                output_unit((3,), unit)
                return 0

            lax.fori_loop(far_first, far_last, far, 0)

        @pl.when(j == 3)
        def _():
            PD[1, 0] = pd_sum(0)
            for i in range(3):
                pd_send(1, i).start()

        @pl.when(j == 4)
        def _():
            DT[...] = pd_sum(1).astype(BF)

        @pl.when(j >= CLASS_LAG)
        def _():
            input_class(j - CLASS_LAG)

        @pl.when(j >= END_LAG)
        def _():
            input_end(j - END_LAG)

        @pl.when(j == 8)
        def _():
            PU[0] = lax.fori_loop(0, UNITS, up_unit, jnp.zeros((16, TOK), F32))
            for i in range(1, 8):
                pu_send(i).start()
            for i in range(1, 4):
                GDs[i - 1] = nn(DT[...], H[:, window(mod(y + i, 4))]).astype(BF)
                gy_send(0, i).start()

        @pl.when(j == 9)
        def _():
            total = PU[0]
            for i in range(1, 8):
                got(PU.at[i], pur.at[i - 1])
                total = total + PU[i]
            UT[...] = total.astype(BF)
            for i in range(1, 4):
                GUs[i - 1] = nn(UT[...], G[:, cols_of(mod(y + i, 4))]).astype(BF)
                gy_send(1, i).start()

        @pl.when(j == 11)
        def _():
            total_down = nn(DT[...], H[:, window(y)])
            total_up = nn(UT[...], G[:, my_cols])
            for i in range(1, 4):
                got(GDr.at[i - 1], gyr.at[0, i - 1])
                got(GUr.at[i - 1], gyr.at[1, i - 1])
                total_down = total_down + GDr[i - 1].astype(F32)
                total_up = total_up + GUr[i - 1].astype(F32)
            gd[...] = total_down * (2.0 / 1024)
            gu[...] = total_up * (2.0 / 1024)

        return 0

    lax.fori_loop(0, UNITS, loop, 0)

    def over(first, last, work):
        def body(unit, _):
            work(unit)
            return 0

        lax.fori_loop(first, last, body, 0)

    def last_unit(unit):
        input_unit(unit)
        output_unit((3,), unit)

    over(UNITS - 2, UNITS, last_unit)
    ox_go(1)
    over(UNITS - CLASS_LAG, UNITS - 1, input_class)
    ox_sum(0)
    over(UNITS - 1, UNITS, input_class)
    over(UNITS - END_LAG, UNITS - 1, input_end)
    ox_sum(1)
    over(UNITS - 1, UNITS, input_end)

    left(G.at[mine, :], gzs)
    for which in range(2):
        left(G.at[0:112, :], gxs.at[which])
    left(PU.at[1:8], pus)
    for i in range(3):
        for stage in range(2):
            pd_send(stage, i).wait_send()
            gy_send(stage, i + 1).wait_send()
        left(I.at[0:64, :], r1s.at[i])
        left(I.at[0:16, :], r2s.at[i])
    left(H.at[0:128, :], hs.at[0])
    left(H.at[0:112, :], hs.at[1])
    for side in range(2):
        left(W.at[:, 0:256], wds.at[side])
        left(W.at[0:FF // 2, 0:256], wfs.at[side])
    left(OXn.at[1:8], oxs.at[0])
    left(OXf.at[1:8], oxs.at[1])
    for far in range(2):
        op_end(far)
        op_send(far).wait_send()


def shards(hidden, out_grad, weight, adapter_down_factor, adapter_up_factor):
    any_spec = pl.BlockSpec(memory_space=pl.ANY)
    vmem_spec = pl.BlockSpec(memory_space=pltpu.VMEM)
    dma = pltpu.SemaphoreType.DMA
    hg, rec, gd, gu = pl.pallas_call(
        kernel,
        out_shape=(
            jax.ShapeDtypeStruct((16, FF), BF),
            jax.ShapeDtypeStruct((16, 2048), BF),
            jax.ShapeDtypeStruct((16, WIN), F32),
            jax.ShapeDtypeStruct((16, 256), F32),
        ),
        in_specs=[any_spec] * 5,
        out_specs=(vmem_spec,) * 4,
        scratch_shapes=[
            pltpu.VMEM((FF, FEAT), BF),
            pltpu.VMEM((TOK, FF), BF),
            pltpu.VMEM((TOK, FEAT), BF),
            pltpu.VMEM((TOK, FF), BF),
            pltpu.VMEM((TOK, FEAT), F32),
            pltpu.VMEM((TOK, FEAT), BF),
            pltpu.VMEM((3, 64, FF), BF),
            pltpu.VMEM((3, 16, FF), BF),
            pltpu.VMEM((16, FF), BF),
            pltpu.VMEM((16, FEAT), BF),
            pltpu.VMEM((2, 4, 16, TOK), F32),
            pltpu.VMEM((8, 16, TOK), F32),
            pltpu.VMEM((16, TOK), BF),
            pltpu.VMEM((16, TOK), BF),
            pltpu.VMEM((3, 16, WIN), BF),
            pltpu.VMEM((3, 16, WIN), BF),
            pltpu.VMEM((3, 16, 256), BF),
            pltpu.VMEM((3, 16, 256), BF),
            pltpu.VMEM((8, 2, 16, 768), BF),
            pltpu.VMEM((8, 2, 16, 256), BF),
            pltpu.VMEM((16, FEAT), BF),
            pltpu.VMEM((16, FEAT), BF),
            dma((11,)),
            dma((2,)), dma((2, UNITS)),
            dma((2,)), dma((2, UNITS)),
            dma((2,)), dma((2, 8)),
            dma, dma,
            dma((2,)), dma((2,)),
            dma((2, 3)), dma((2, 3)),
            dma, dma((7,)),
            dma((2, 3)), dma((2, 3)),
            dma((3,)), dma((3, UNITS)),
            dma((3,)), dma((3, UNITS)),
            dma((2,)), dma((2,)),
            dma((2,)), dma((2,)),
        ],
        compiler_params=pltpu.CompilerParams(
            collective_id=0, has_side_effects=True, vmem_limit_bytes=63 * 1024 * 1024
        ),
    )(hidden, out_grad, weight, adapter_down_factor.T, adapter_up_factor)
    offset = lax.rem(lax.axis_index("gz"), 4) * 32
    grad_down = lax.dynamic_slice_in_dim(gd, offset, FF // 8, 1).T
    return hg, rec, grad_down, gu


def solution(mesh):
    placed = (
        P(("gz", "gy"), "gx"),
        P(("gz", "gx"), "gy"),
        P("gx", ("gy", "gz")),
        P("gx", None),
        P(None, "gy"),
    )
    return jax.shard_map(
        shards,
        mesh=mesh,
        in_specs=placed,
        out_specs=(
            P(("gz", "gy"), "gx"),
            P(("gz", "gx"), "gy"),
            P(("gx", "gz"), None),
            P(None, ("gy", "gz")),
        ),
        check_vma=False,
    )
```

time: 813 us -> 111 us (0.14)
  the two profiles are of different devices: /device:TPU:1 before, /device:TPU:32 now
where the time goes in v2:
time: 111 us
  Pallas kernels  104 us (94%)
  local copies, waits for them, and re-layouts  5.8 us (5%)
    pallas_call x1, Pallas kernels, shards(): pl.pallas_call(kernel, out_shape=(jax.ShapeDtypeStruct((16, FF), BF), jax...  104 us
    unnamed x3, local copies, waits for them, and re-layouts  4.34 us

profile of v2, /device:TPU:32, one launch (start us, length us, event | category | flops | bytes accessed | tf_op | source)
XLA Modules:
  0.0 110.8 jit_solution(12449470720136984447)
XLA Ops:
  0.6 104.3 %shard_map.84 = (bf16[16,3328]{1,0:T(8,128)(2,1)}, bf16[16,2048]{1,0:T(8,128)(2,1)}, f32[16,512]{1,0:T(8,128)}, f32[16,256]{1,0:T(8,128)}) custom-call(bf16[16,3328]{1,0:T(8,128)(2,1)} %hid.1, bf16[16,2048]{1,0:T(8,128)(2,1)} %og.1, bf16[3328,256]{1,0:T(8,128)(2,1)} %w.1, bf16[16,3328]{1,0:T(8,128)(2,1)} %bitcast.3, bf16[16,2048]{1,0:T(8,128)(2,1)} %au.1), custom_call_target="tpu_custom_call" | custom-call | tf_op jit(solution)/shard_map/pallas_call | solution.py:452
  105.0 1.5 %dynamic-slice_bitcast_fusion = f32[416,16]{0,1:T(8,128)} fusion(f32[16,512]{1,0:T(8,128)} %get-tuple-element.10, s32[]{:T(128)S(6)} %select_n.3), kind=kLoop, calls=%fused_computation | loop fusion | bytes 53252 | tf_op jit(solution)/shard_map/transpose | solution.py:504
  106.4 1.5 %copy.12 = bf16[16,3328]{1,0:T(8,128)(2,1)} copy(bf16[16,3328]{1,0:T(8,128)(2,1)} %get-tuple-element.16) | data formatting | bytes 212992
  108.0 1.5 %copy.13 = bf16[16,2048]{1,0:T(8,128)(2,1)} copy(bf16[16,2048]{1,0:T(8,128)(2,1)} %get-tuple-element.17) | data formatting | bytes 131072
  109.4 1.3 %copy.14 = f32[16,256]{1,0:T(8,128)} copy(f32[16,256]{1,0:T(8,128)} %get-tuple-element.19) | data formatting | bytes 32768

commit v3 on v2

--- a/solution.py
+++ b/solution.py
@@ -14,12 +14,15 @@
 FF = 3328
 UNIT = 256
 UNITS = FF // UNIT
-HALF = UNIT // 2
+CHUNK = 128
+CHUNKS = FF // CHUNK
+HALF = CHUNK // 2
 TOK = 256
 FEAT = 1024
-AHEAD = 4
-CLASS_LAG = 5
+AHEAD = 5
+CLASS_LEFT = 3
 END_LAG = 8
+H_LAG = 1
 WIN = 512
 
 
@@ -46,7 +49,7 @@
 def kernel(
     hid, og, w, adt, au,
     hg, rec, gd, gu,
-    W, H, G, I, O, Ob, R1, R2, ADT, AU, PD, PU, DT, UT, GDs, GDr, GUs, GUr, OXn, OXf, OPs, OPr,
+    W, H, G, I, O, Ob, R1, R2, ADT, AU, PD, PU, DT, UT, GDs, GDr, GUs, GUr, OXn, OXf, OPs, OPr, LOW, LOWO,
     lsem, wds, wdr, wfs, wfr, hs, hr, gzs, gzr, gxs, gxr, pds, pdr, pus, pur, gys, gyr,
     r1s, r1r, r2s, r2r, oxs, oxr, ops_, opr,
 ):
@@ -113,12 +116,15 @@
     def w_rows(unit):
         return pl.ds(pl.multiple_of(unit * UNIT, UNIT), UNIT)
 
-    def w_half(unit, side):
-        return pl.ds(pl.multiple_of(unit * UNIT + side * HALF, HALF), HALF)
+    def w_chunk(chunk):
+        return pl.ds(pl.multiple_of(chunk * CHUNK, CHUNK), CHUNK)
+
+    def w_half(chunk, side):
+        return pl.ds(pl.multiple_of(chunk * CHUNK + side * HALF, HALF), HALF)
 
     def w_direct(unit, side):
         return remote(
-            w.at[w_rows(unit), :], W.at[w_rows(unit), my_cols], wds.at[side], wdr.at[side, unit],
+            w.at[w_chunk(unit), :], W.at[w_chunk(unit), my_cols], wds.at[side], wdr.at[side, unit],
             ydev(yup if side == 0 else ydown),
         )
 
@@ -127,13 +133,13 @@
         return remote(part, part, wfs.at[side], wfr.at[side, unit], ydev(yup if side == 0 else ydown))
 
     def w_step(unit):
-        @pl.when(unit + AHEAD < UNITS)
+        @pl.when(unit + AHEAD < CHUNKS)
         def _():
             w_direct(unit + AHEAD, 0).start()
             w_direct(unit + AHEAD, 1).start()
 
         for side in range(2):
-            got(W.at[w_rows(unit), cols_of(ydown if side == 0 else yup)], wdr.at[side, unit])
+            got(W.at[w_chunk(unit), cols_of(ydown if side == 0 else yup)], wdr.at[side, unit])
             w_pass(unit, side).start()
 
     for unit in range(AHEAD):
@@ -183,7 +189,7 @@
     def pd_sum(stage):
         for i in range(3):
             got(PD.at[stage, i + 1], pdr.at[stage, i])
-        return PD[stage, 0] + PD[stage, 1] + PD[stage, 2] + PD[stage, 3]
+        return sum(PD[stage, i].astype(F32) for i in range(4))
 
     def pu_send(i):
         return remote(PU.at[0], PU.at[i], pus, pur.at[i - 1], xdev(i))
@@ -216,7 +222,8 @@
 
     def input_unit(unit):
         for side in range(2):
-            got(W.at[w_half(unit, side), cols_of(yfar)], wfr.at[side, unit])
+            for chunk in (2 * unit, 2 * unit + 1):
+                got(W.at[w_half(chunk, side), cols_of(yfar)], wfr.at[side, chunk])
         I[:, unit_cols(unit)] = nt(G[...], W[w_rows(unit), :]).astype(BF)
         for i in range(3):
             r1_send(unit, i).start()
@@ -245,8 +252,7 @@
         total = R1[0, rows16(zm), cols].astype(F32)
         for i in range(3):
             total = total + R2[i, :, cols].astype(F32)
-        low = nt(pick(z), DT[...]).astype(BF)
-        hg[:, cols] = (total + 2.0 * nn(low, ADT[:, cols])).astype(BF)
+        hg[:, cols] = (total + LOW[:, cols]).astype(BF)
 
     order = (0, 1, 3, 2)
 
@@ -280,11 +286,9 @@
             total = O[rows_of(half * 8 + gx), lo:hi]
             for i in range(1, 8):
                 total = total + OX[i, half].astype(F32)
-            low = nt(pick(half * 8 + gx), UT[...]).astype(BF)
+            total = (total + LOWO[which, :, lo:hi]).astype(BF)
             for q in range(lo // 256, hi // 256):
-                factor = AU[:, cols_of(mod(y + order[q], 4))]
                 part = total[:, q * 256 - lo:(q + 1) * 256 - lo]
-                part = (part + 2.0 * nn(low, factor)).astype(BF)
                 if which == 0:
                     OPs[:, q * 256:(q + 1) * 256] = part
                 else:
@@ -299,9 +303,11 @@
             rec[:, quarter(mod(y + order[q], 4), 1 - zh)] = OPr[:, q * 256:(q + 1) * 256]
 
     def loop(j, _):
-        @pl.when(j < 8)
-        def _():
-            h_step(j)
+        w_step(2 * j)
+
+        @pl.when((j >= H_LAG) & (j < 8 + H_LAG))
+        def _():
+            h_step(j - H_LAG)
 
         @pl.when(j == 1)
         def _():
@@ -309,20 +315,20 @@
             for i in range(1, 8):
                 g_send(i, theirs, 1).start()
 
-        w_step(j)
+        w_step(2 * j + 1)
 
         @pl.when(j == 2)
         def _():
             for which in range(2):
                 got(G.at[0:112, :], gxr.at[which])
-            PD[0, 0] = nt(AU[...], G[...])
+            PD[0, 0] = nt(AU[...], G[...]).astype(BF)
             for i in range(3):
                 pd_send(0, i).start()
 
-        first = lax.min(3 * (j - 8), UNITS - 1)
-        last = lax.min(3 * (j - 7), UNITS)
-
-        @pl.when(j >= 8)
+        first = lax.min(4 * (j - 9), UNITS - 1)
+        last = lax.min(4 * (j - 8), UNITS)
+
+        @pl.when(j >= 9)
         def _():
             def near(unit, _):
                 output_unit((0, 1, 2), unit)
@@ -351,7 +357,7 @@
 
         @pl.when(j == 3)
         def _():
-            PD[1, 0] = pd_sum(0)
+            PD[1, 0] = pd_sum(0).astype(BF)
             for i in range(3):
                 pd_send(1, i).start()
 
@@ -359,15 +365,21 @@
         def _():
             DT[...] = pd_sum(1).astype(BF)
 
-        @pl.when(j >= CLASS_LAG)
-        def _():
-            input_class(j - CLASS_LAG)
+        def classes(turn):
+            late = (turn >= 10).astype(jnp.int32) + (turn >= 12).astype(jnp.int32)
+            return lax.max(turn - 4 + late, 0)
+
+        def class_body(unit, _):
+            input_class(unit)
+            return 0
+
+        lax.fori_loop(classes(j - 1), classes(j), class_body, 0)
 
         @pl.when(j >= END_LAG)
         def _():
             input_end(j - END_LAG)
 
-        @pl.when(j == 8)
+        @pl.when(j == 8 + H_LAG)
         def _():
             PU[0] = lax.fori_loop(0, UNITS, up_unit, jnp.zeros((16, TOK), F32))
             for i in range(1, 8):
@@ -376,7 +388,7 @@
                 GDs[i - 1] = nn(DT[...], H[:, window(mod(y + i, 4))]).astype(BF)
                 gy_send(0, i).start()
 
-        @pl.when(j == 9)
+        @pl.when(j == 9 + H_LAG)
         def _():
             total = PU[0]
             for i in range(1, 8):
@@ -387,7 +399,19 @@
                 GUs[i - 1] = nn(UT[...], G[:, cols_of(mod(y + i, 4))]).astype(BF)
                 gy_send(1, i).start()
 
-        @pl.when(j == 11)
+        @pl.when(j == 5)
+        def _():
+            low = nt(pick(z), DT[...]).astype(BF)
+            LOW[...] = 2.0 * nn(low, ADT[...])
+
+        @pl.when(j == 10 + H_LAG)
+        def _():
+            for which, half in ((0, 1 - zh), (1, zh)):
+                low = nt(pick(half * 8 + gx), UT[...]).astype(BF)
+                for q in range(4):
+                    LOWO[which, :, q * 256:(q + 1) * 256] = 2.0 * nn(low, AU[:, cols_of(mod(y + order[q], 4))])
+
+        @pl.when(j == 11 + H_LAG)
         def _():
             total_down = nn(DT[...], H[:, window(y)])
             total_up = nn(UT[...], G[:, my_cols])
@@ -416,12 +440,11 @@
 
     over(UNITS - 2, UNITS, last_unit)
     ox_go(1)
-    over(UNITS - CLASS_LAG, UNITS - 1, input_class)
+    over(UNITS - CLASS_LEFT, UNITS - 1, input_class)
     ox_sum(0)
     over(UNITS - 1, UNITS, input_class)
+    ox_sum(1)
     over(UNITS - END_LAG, UNITS - 1, input_end)
-    ox_sum(1)
-    over(UNITS - 1, UNITS, input_end)
 
     left(G.at[mine, :], gzs)
     for which in range(2):
@@ -440,9 +463,21 @@
         left(W.at[0:FF // 2, 0:256], wfs.at[side])
     left(OXn.at[1:8], oxs.at[0])
     left(OXf.at[1:8], oxs.at[1])
+    over(UNITS - 1, UNITS, input_end)
     for far in range(2):
         op_end(far)
         op_send(far).wait_send()
+
+
+def hand_over(hg_in, rec_in, gd_in, gu_in, hg, rec, gd, gu):
+    hg[...] = hg_in[...]
+    rec[...] = rec_in[...]
+    gu[...] = gu_in[...]
+    place = lax.rem(lax.axis_index("gz"), 4)
+    for k in range(4):
+        @pl.when(place == k)
+        def _(k=k):
+            gd[...] = gd_in[:, 32 * k:32 * k + FF // 8]
 
 
 def shards(hidden, out_grad, weight, adapter_down_factor, adapter_up_factor):
@@ -470,7 +505,7 @@
             pltpu.VMEM((3, 16, FF), BF),
             pltpu.VMEM((16, FF), BF),
             pltpu.VMEM((16, FEAT), BF),
-            pltpu.VMEM((2, 4, 16, TOK), F32),
+            pltpu.VMEM((2, 4, 16, TOK), BF),
             pltpu.VMEM((8, 16, TOK), F32),
             pltpu.VMEM((16, TOK), BF),
             pltpu.VMEM((16, TOK), BF),
@@ -482,9 +517,11 @@
             pltpu.VMEM((8, 2, 16, 256), BF),
             pltpu.VMEM((16, FEAT), BF),
             pltpu.VMEM((16, FEAT), BF),
+            pltpu.VMEM((16, FF), F32),
+            pltpu.VMEM((2, 16, FEAT), F32),
             dma((11,)),
-            dma((2,)), dma((2, UNITS)),
-            dma((2,)), dma((2, UNITS)),
+            dma((2,)), dma((2, CHUNKS)),
+            dma((2,)), dma((2, CHUNKS)),
             dma((2,)), dma((2, 8)),
             dma, dma,
             dma((2,)), dma((2,)),
@@ -500,9 +537,18 @@
             collective_id=0, has_side_effects=True, vmem_limit_bytes=63 * 1024 * 1024
         ),
     )(hidden, out_grad, weight, adapter_down_factor.T, adapter_up_factor)
-    offset = lax.rem(lax.axis_index("gz"), 4) * 32
-    grad_down = lax.dynamic_slice_in_dim(gd, offset, FF // 8, 1).T
-    return hg, rec, grad_down, gu
+    hg, rec, gd, gu = pl.pallas_call(
+        hand_over,
+        out_shape=(
+            jax.ShapeDtypeStruct((16, FF), BF),
+            jax.ShapeDtypeStruct((16, 2048), BF),
+            jax.ShapeDtypeStruct((16, FF // 8), F32),
+            jax.ShapeDtypeStruct((16, 256), F32),
+        ),
+        in_specs=[vmem_spec] * 4,
+        out_specs=(vmem_spec,) * 4,
+    )(hg, rec, gd, gu)
+    return hg, rec, gd.T, gu
 
 
 def solution(mesh):

time: 111 us -> 101 us (0.910)
  the two profiles are of different devices: /device:TPU:32 before, /device:TPU:1 now
where the time goes in v3:
time: 101 us; the launch traced here: 99.7 us
  Pallas kernels  99 us (98%)
    pallas_call x1, Pallas kernels, shards(): pl.pallas_call(kernel, out_shape=(jax.ShapeDtypeStruct((16, FF), BF), jax...  97.4 us

profile of v3, /device:TPU:1, one launch (start us, length us, event | category | flops | bytes accessed | tf_op | source)
XLA Modules:
  0.0 99.7 jit_solution(8892228020624142683)
XLA Ops:
  0.6 97.4 %shard_map.84 = (bf16[16,3328]{1,0:T(8,128)(2,1)}, bf16[16,2048]{1,0:T(8,128)(2,1)}, f32[16,512]{1,0:T(8,128)}, f32[16,256]{1,0:T(8,128)}) custom-call(bf16[16,3328]{1,0:T(8,128)(2,1)} %hid.1, bf16[16,2048]{1,0:T(8,128)(2,1)} %og.1, bf16[3328,256]{1,0:T(8,128)(2,1)} %w.1, bf16[16,3328]{1,0:T(8,128)(2,1)} %bitcast.2, bf16[16,2048]{1,0:T(8,128)(2,1)} %au.1), custom_call_target="tpu_custom_call" | custom-call | tf_op jit(solution)/shard_map/pallas_call | solution.py:487
  98.0 1.6 %shard_map.85 = (bf16[16,3328]{1,0:T(8,128)(2,1)}, bf16[16,2048]{1,0:T(8,128)(2,1)}, f32[16,416]{1,0:T(8,128)}, f32[16,256]{1,0:T(8,128)}) custom-call(bf16[16,3328]{1,0:T(8,128)(2,1)} %get-tuple-element.12.hg_in, bf16[16,2048]{1,0:T(8,128)(2,1)} %get-tuple-element.13.rec_in, f32[16,512]{1,0:T(8,128)} %get-tuple-element.14.gd_in, ...), custom_call_target="tpu_custom_call" | custom-call | tf_op jit(solution)/shard_map/pallas_call | solution.py:540

commit v4 on v3

--- a/solution.py
+++ b/solution.py
@@ -325,6 +325,10 @@
             for i in range(3):
                 pd_send(0, i).start()
 
+        @pl.when(j >= 2)
+        def _():
+            input_unit(j - 2)
+
         first = lax.min(4 * (j - 9), UNITS - 1)
         last = lax.min(4 * (j - 8), UNITS)
 
@@ -339,10 +343,6 @@
         @pl.when(j == UNITS - 1)
         def _():
             ox_go(0)
-
-        @pl.when(j >= 2)
-        def _():
-            input_unit(j - 2)
 
         far_first = lax.min(4 * (j - 9), j - 2)
         far_last = lax.min(4 * (j - 8), j - 1)
@@ -386,7 +386,6 @@
                 pu_send(i).start()
             for i in range(1, 4):
                 GDs[i - 1] = nn(DT[...], H[:, window(mod(y + i, 4))]).astype(BF)
-                gy_send(0, i).start()
 
         @pl.when(j == 9 + H_LAG)
         def _():
@@ -397,7 +396,6 @@
             UT[...] = total.astype(BF)
             for i in range(1, 4):
                 GUs[i - 1] = nn(UT[...], G[:, cols_of(mod(y + i, 4))]).astype(BF)
-                gy_send(1, i).start()
 
         @pl.when(j == 5)
         def _():
@@ -411,18 +409,6 @@
                 for q in range(4):
                     LOWO[which, :, q * 256:(q + 1) * 256] = 2.0 * nn(low, AU[:, cols_of(mod(y + order[q], 4))])
 
-        @pl.when(j == 11 + H_LAG)
-        def _():
-            total_down = nn(DT[...], H[:, window(y)])
-            total_up = nn(UT[...], G[:, my_cols])
-            for i in range(1, 4):
-                got(GDr.at[i - 1], gyr.at[0, i - 1])
-                got(GUr.at[i - 1], gyr.at[1, i - 1])
-                total_down = total_down + GDr[i - 1].astype(F32)
-                total_up = total_up + GUr[i - 1].astype(F32)
-            gd[...] = total_down * (2.0 / 1024)
-            gu[...] = total_up * (2.0 / 1024)
-
         return 0
 
     lax.fori_loop(0, UNITS, loop, 0)
@@ -438,6 +424,9 @@
         input_unit(unit)
         output_unit((3,), unit)
 
+    for i in range(1, 4):
+        gy_send(0, i).start()
+        gy_send(1, i).start()
     over(UNITS - 2, UNITS, last_unit)
     ox_go(1)
     over(UNITS - CLASS_LEFT, UNITS - 1, input_class)
@@ -445,6 +434,15 @@
     over(UNITS - 1, UNITS, input_class)
     ox_sum(1)
     over(UNITS - END_LAG, UNITS - 1, input_end)
+    total_down = nn(DT[...], H[:, window(y)])
+    total_up = nn(UT[...], G[:, my_cols])
+    for i in range(1, 4):
+        got(GDr.at[i - 1], gyr.at[0, i - 1])
+        got(GUr.at[i - 1], gyr.at[1, i - 1])
+        total_down = total_down + GDr[i - 1].astype(F32)
+        total_up = total_up + GUr[i - 1].astype(F32)
+    gd[...] = total_down * (2.0 / 1024)
+    gu[...] = total_up * (2.0 / 1024)
 
     left(G.at[mine, :], gzs)
     for which in range(2):

time: 101 us -> 99.7 us (0.987)
  no operation moved by 1% of the time
where the time goes in v4:
time: 99.7 us; the launch traced here: 99.1 us
  Pallas kernels  98.5 us (99%)
    pallas_call x1, Pallas kernels, shards(): pl.pallas_call(kernel, out_shape=(jax.ShapeDtypeStruct((16, FF), BF), jax...  96.9 us

profile of v4, /device:TPU:1, one launch (start us, length us, event | category | flops | bytes accessed | tf_op | source)
XLA Modules:
  0.0 99.1 jit_solution(8889383122920564917)
XLA Ops:
  0.6 96.9 %shard_map.84 = (bf16[16,3328]{1,0:T(8,128)(2,1)}, bf16[16,2048]{1,0:T(8,128)(2,1)}, f32[16,512]{1,0:T(8,128)}, f32[16,256]{1,0:T(8,128)}) custom-call(bf16[16,3328]{1,0:T(8,128)(2,1)} %hid.1, bf16[16,2048]{1,0:T(8,128)(2,1)} %og.1, bf16[3328,256]{1,0:T(8,128)(2,1)} %w.1, bf16[16,3328]{1,0:T(8,128)(2,1)} %bitcast.2, bf16[16,2048]{1,0:T(8,128)(2,1)} %au.1), custom_call_target="tpu_custom_call" | custom-call | tf_op jit(solution)/shard_map/pallas_call | solution.py:485
  97.5 1.6 %shard_map.85 = (bf16[16,3328]{1,0:T(8,128)(2,1)}, bf16[16,2048]{1,0:T(8,128)(2,1)}, f32[16,416]{1,0:T(8,128)}, f32[16,256]{1,0:T(8,128)}) custom-call(bf16[16,3328]{1,0:T(8,128)(2,1)} %get-tuple-element.12.hg_in, bf16[16,2048]{1,0:T(8,128)(2,1)} %get-tuple-element.13.rec_in, f32[16,512]{1,0:T(8,128)} %get-tuple-element.14.gd_in, ...), custom_call_target="tpu_custom_call" | custom-call | tf_op jit(solution)/shard_map/pallas_call | solution.py:538

commit v5 on v4

--- a/solution.py
+++ b/solution.py
@@ -14,12 +14,12 @@
 FF = 3328
 UNIT = 256
 UNITS = FF // UNIT
-CHUNK = 128
+CHUNK = 64
 CHUNKS = FF // CHUNK
 HALF = CHUNK // 2
 TOK = 256
 FEAT = 1024
-AHEAD = 5
+AHEAD = 10
 CLASS_LEFT = 3
 END_LAG = 8
 H_LAG = 1
@@ -222,7 +222,8 @@
 
     def input_unit(unit):
         for side in range(2):
-            for chunk in (2 * unit, 2 * unit + 1):
+            for part in range(4):
+                chunk = 4 * unit + part
                 got(W.at[w_half(chunk, side), cols_of(yfar)], wfr.at[side, chunk])
         I[:, unit_cols(unit)] = nt(G[...], W[w_rows(unit), :]).astype(BF)
         for i in range(3):
@@ -303,7 +304,8 @@
             rec[:, quarter(mod(y + order[q], 4), 1 - zh)] = OPr[:, q * 256:(q + 1) * 256]
 
     def loop(j, _):
-        w_step(2 * j)
+        w_step(4 * j)
+        w_step(4 * j + 1)
 
         @pl.when((j >= H_LAG) & (j < 8 + H_LAG))
         def _():
@@ -315,7 +317,8 @@
             for i in range(1, 8):
                 g_send(i, theirs, 1).start()
 
-        w_step(2 * j + 1)
+        w_step(4 * j + 2)
+        w_step(4 * j + 3)
 
         @pl.when(j == 2)
         def _():

time: 99.7 us -> 102 us (1.023)
  Pallas kernels: 98.5 us -> 101 us
    pallas_call x1, Pallas kernels: 96.9 us -> 99.1 us  [shards(): pl.pallas_call(kernel, out_shape=(jax.ShapeDtypeStruct((16, FF), BF), jax...]
where the time goes in v5:
time: 102 us; the launch traced here: 101 us
  Pallas kernels  101 us (99%)
    pallas_call x1, Pallas kernels, shards(): pl.pallas_call(kernel, out_shape=(jax.ShapeDtypeStruct((16, FF), BF), jax...  99.1 us

profile of v5, /device:TPU:1, one launch (start us, length us, event | category | flops | bytes accessed | tf_op | source)
XLA Modules:
  0.0 101.4 jit_solution(9690321984365080657)
XLA Ops:
  0.6 99.1 %shard_map.84 = (bf16[16,3328]{1,0:T(8,128)(2,1)}, bf16[16,2048]{1,0:T(8,128)(2,1)}, f32[16,512]{1,0:T(8,128)}, f32[16,256]{1,0:T(8,128)}) custom-call(bf16[16,3328]{1,0:T(8,128)(2,1)} %hid.1, bf16[16,2048]{1,0:T(8,128)(2,1)} %og.1, bf16[3328,256]{1,0:T(8,128)(2,1)} %w.1, bf16[16,3328]{1,0:T(8,128)(2,1)} %bitcast.2, bf16[16,2048]{1,0:T(8,128)(2,1)} %au.1), custom_call_target="tpu_custom_call" | custom-call | tf_op jit(solution)/shard_map/pallas_call | solution.py:488
  99.7 1.6 %shard_map.85 = (bf16[16,3328]{1,0:T(8,128)(2,1)}, bf16[16,2048]{1,0:T(8,128)(2,1)}, f32[16,416]{1,0:T(8,128)}, f32[16,256]{1,0:T(8,128)}) custom-call(bf16[16,3328]{1,0:T(8,128)(2,1)} %get-tuple-element.12.hg_in, bf16[16,2048]{1,0:T(8,128)(2,1)} %get-tuple-element.13.rec_in, f32[16,512]{1,0:T(8,128)} %get-tuple-element.14.gd_in, ...), custom_call_target="tpu_custom_call" | custom-call | tf_op jit(solution)/shard_map/pallas_call | solution.py:541
